TPU v7x, 256 devices: a whole 4x4x8 slice. The times are simulated.
256 devices in a mesh: proto: 64 (over z, x, core), view: 4 (over y).
Axes of the slice: x: 4, y: 4, z: 8, core: 2. Of those that a mesh axis runs over, the one named last changes fastest.
Arguments:
- features: float32 [6144, 2, 256], P(('view', 'proto')), may hold values from -6 to 6
- prototypes: float32 [65536, 256], P('proto'), may hold values from -6 to 6
- code_counts: int32 [6144, 2, 65536], P('view', None, 'proto'), may hold values from 0 to 1023
Outputs:
- features_grad: float32 [6144, 2, 256], P(('view', 'proto'))
- proto_grad: float32 [65536, 256], P('proto')
All inputs are finite; a program needn't handle non-finite values.
Results may differ from a plain program's by a relative error of at most 0.0003.
Values sent between devices are 32-bit elements; how exact they have to be, the bound alone decides.
A program may use at most 128 MiB of HBM per device.

v0:
```python
import jax
import jax.numpy as jnp
from jax import lax
from jax.sharding import PartitionSpec as P

SOFTMAX_TEMP = 0.1
SCALE_OF_LOSS = 4096.0
FIXED_POINT = 2.0 ** (-24)


def per_device(features, prototypes, code_counts):
    largest_logit = lax.Precision.HIGHEST
    weight_factor = SCALE_OF_LOSS / SOFTMAX_TEMP
    feature_norm = jnp.sqrt(jnp.sum(features * features, axis=2, keepdims=True) + 1e-06)
    unit = features / feature_norm
    proto_norm = jnp.sqrt(jnp.sum(prototypes * prototypes, axis=1, keepdims=True) + 1e-06)
    cluster_center = prototypes / proto_norm
    collected_rows = lax.all_gather(unit, "proto", axis=0, tiled=True)
    score_matrix = (
        jnp.einsum("vhf,xf->vhx", collected_rows, cluster_center, precision=largest_logit)
        / SOFTMAX_TEMP
    )
    exponent = jnp.exp(score_matrix)
    swapped = code_counts[:, ::-1, :].astype(jnp.float32) * FIXED_POINT
    local_totals = jnp.sum(exponent, axis=2)
    local_masses = jnp.sum(swapped, axis=2)
    totals, masses = lax.psum((local_totals, local_masses), "proto")
    gradient = weight_factor * ((masses / totals)[:, :, None] * exponent - swapped)
    unit_grad = lax.psum_scatter(
        jnp.einsum("bjk,kd->bjd", gradient, cluster_center, precision=largest_logit),
        "proto",
        scatter_dimension=0,
        tiled=True,
    )
    partial_grad = jnp.einsum("bjk,bjd->kd", gradient, collected_rows, precision=largest_logit)
    proto_grad = lax.psum(partial_grad, "view")
    inner_product = jnp.sum(unit * unit_grad, axis=2, keepdims=True)
    features_grad = (unit_grad - unit * inner_product) / feature_norm
    return (features_grad, proto_grad)


def solution(mesh):
    in_specs = (P(("view", "proto"), None, None), P("proto", None), P("view", None, "proto"))
    out_specs = (P(("view", "proto"), None, None), P("proto", None))
    return jax.shard_map(
        per_device, mesh=mesh, in_specs=in_specs, out_specs=out_specs, check_vma=False
    )
```

profile of v0, /device:TPU:8, one launch (start us, length us, event | category | flops | bytes accessed | tf_op | source)
XLA Modules:
  0.0 593.7 jit_solution(11057192030614561602)
XLA Ops:
  7.2 0.0 all-gather.2.cloned.1.call-start
  7.2 0.9 multiply_reduce_fusion.1
  8.1 0.1 copy.15
  8.2 1.5 copy_divide_fusion
  9.7 0.0 all-gather.2.cloned.1.call-update
  9.7 0.0 copy-start.2
  9.7 0.0 reduce-scatter.2.cloned.1.call-start
  9.8 19.2 %copy.14 = s32[1536,2,1024]{0,2,1:T(8,128)} copy(s32[1536,2,1024]{2,1,0:T(2,128)} %param.5) | data formatting | bytes 25165824 | tf_op args[2]
  29.0 0.0 copy-done.2
  29.0 0.2 multiply_reduce_fusion
  29.3 6.1 %fusion.1 = f32[1536,2]{0,1:T(2,128)S(1)} fusion(s32[1536,2,1024]{0,2,1:T(8,128)} %copy.14), kind=kLoop, calls=%fused_computation.4 | loop fusion | flops 9434112 | bytes 12595200 | tf_op jit(solution)/shard_map/reduce_sum | solution.py:26
  35.4 57.1 %all-gather.2.cloned.1.call-done = f32[1536,2,256]{2,0,1:T(8,128)} async-done(((f32[24,2,256]{2,0,1:T(8,128)}), f32[1536,2,256]{2,0,1:T(8,128)}) %all-gather.2.cloned.1.call-update) | async-done | bytes 3145744 | tf_op jit(solution)/shard_map/all_gather | solution.py:18
  92.5 15.0 %fusion.2 = (f32[1536,2]{0,1:T(2,128)S(1)}, f32[1536,2,1024]{0,2,1:T(8,128)}) fusion(f32[1536,2,256]{2,0,1:T(8,128)} %all-gather.2.cloned.1.call-done, f32[1024,256]{1,0:T(8,128)S(1)} %copy-done.2, f32[1024]{0:T(1024)S(1)} %add_sqrt_fusion), kind=kOutput, calls=%fused_computation.5 | convolution fusion | flops 9670226944 | bytes 16793600 | tf_op jit(solution)/shard_map/vhf,xf->vhx/dot_general | solution.py:20
  107.5 248.4 %all-reduce = (f32[1536,2]{0,1:T(2,128)S(1)}, f32[1536,2]{0,1:T(2,128)S(1)}) all-reduce(f32[1536,2]{0,1:T(2,128)S(1)} %fusion.1, f32[1536,2]{0,1:T(2,128)S(1)} %get-tuple-element.10), channel_id=1, replica_groups=mesh['proto'=64,'view'=4] {'proto'}, use_global_device_ids=true, to_apply=%region_1.0 | all-reduce | flops 6144 | bytes 49152 | tf_op jit(solution)/shard_map/psum | solution.py:27
  355.9 0.0 copy-start.3
  355.9 9.9 %subtract_multiply_fusion = f32[1536,2,1024]{0,2,1:T(8,128)S(1)} fusion(s32[1536,2,1024]{0,2,1:T(8,128)} %copy.14, f32[1536,2,1024]{0,2,1:T(8,128)} %get-tuple-element.11, f32[1536,2]{0,1:T(2,128)S(1)} %div.37), kind=kLoop, calls=%fused_computation.1 | loop fusion | flops 18874368 | bytes 37761024 | tf_op jit(solution)/shard_map/mul | solution.py:28
  365.9 0.0 copy-start
  365.9 4.6 copy-done
  370.4 0.0 copy-done.3
  370.4 0.0 copy-start.1
  370.4 23.3 %fusion.6 = f32[1536,2,256]{2,0,1:T(8,128)} fusion(f32[1536,2,1024]{0,2,1:T(8,128)S(1)} %subtract_multiply_fusion, f32[1024,256]{1,0:T(8,128)S(1)} %copy-done.3, f32[1024]{0:T(1024)S(1)} %add_sqrt_fusion), kind=kOutput, calls=%fused_computation.10 | convolution fusion | flops 9663938560 | bytes 16781312 | tf_op jit(solution)/shard_map/bjk,kd->bjd/dot_general | solution.py:30
  393.8 0.0 copy-start.4
  393.8 0.0 reduce-scatter.2.cloned.1.call-update
  393.8 0.0 all-reduce.3.cloned.1.call-start
  393.9 0.0 copy-done.1
  393.9 13.9 %convolution_bitcast_fusion = f32[1024,256]{1,0:T(8,128)} fusion(f32[1536,2,1024]{0,2,1:T(8,128)} %copy-done, f32[1536,2,256]{2,0,1:T(8,128)S(1)} %copy-done.1), kind=kOutput, calls=%fused_computation.6 | convolution fusion | flops 9663676416 | bytes 16777216 | tf_op jit(solution)/shard_map/bjk,bjd->kd/dot_general | solution.py:35
  407.7 0.0 all-reduce.3.cloned.1.call-update
  407.8 125.9 %reduce-scatter.2.cloned.1.call-done = f32[24,2,256]{2,0,1:T(8,128)} async-done(((f32[1536,2,256]{2,0,1:T(8,128)}), f32[24,2,256]{2,0,1:T(8,128)}) %reduce-scatter.2.cloned.1.call-update) | async-done | bytes 49168 | tf_op jit(solution)/shard_map/reduce_scatter | solution.py:29
  533.7 0.0 copy-done.4
  533.7 1.0 fusion.5
  534.7 0.6 copy.18
  535.4 49.6 %all-reduce.3.cloned.1.call-done = f32[1024,256]{1,0:T(8,128)} async-done(((f32[1024,256]{1,0:T(8,128)}), f32[1024,256]{1,0:T(8,128)}) %all-reduce.3.cloned.1.call-update) | async-done | bytes 1048592 | tf_op jit(solution)/shard_map/psum | solution.py:36
  584.9 2.3 copy.28
  (3 shorter events, 0.0 us)
Async XLA Ops:
  7.2 85.3 %all-gather.2.cloned.1.call-start = ((), (), s32[]{:S(2)}) async-start(), calls=%async_computation.1 | async-start | bytes 3194880 | tf_op jit(solution)/shard_map/all_gather | solution.py:18
  9.7 19.3 %copy-start.2 = (f32[1024,256]{1,0:T(8,128)S(1)}, f32[1024,256]{1,0:T(8,128)}, u32[]{:S(2)}) copy-start(f32[1024,256]{1,0:T(8,128)} %param.4) | copy-start | bytes 3145732
  9.7 523.9 %reduce-scatter.2.cloned.1.call-start = ((), (), s32[]{:S(2)}) async-start(), calls=%async_computation.2 | async-start | bytes 3194880 | tf_op jit(solution)/shard_map/reduce_scatter | solution.py:29
  355.9 14.5 %copy-start.3 = (f32[1024,256]{1,0:T(8,128)S(1)}, f32[1024,256]{1,0:T(8,128)}, u32[]{:S(2)}) copy-start(f32[1024,256]{1,0:T(8,128)} %param.4) | copy-start | bytes 3145732
  365.9 4.6 copy-start
  370.4 23.4 %copy-start.1 = (f32[1536,2,256]{2,0,1:T(8,128)S(1)}, f32[1536,2,256]{2,0,1:T(8,128)}, u32[]{:S(2)}) copy-start(f32[1536,2,256]{2,0,1:T(8,128)} %all-gather.2.cloned.1.call-done) | copy-start | bytes 9437188
  393.8 139.9 %copy-start.4 = (f32[24,2,256]{2,1,0:T(2,128)S(1)}, f32[24,2,256]{2,1,0:T(2,128)}, u32[]{:S(2)}) copy-start(f32[24,2,256]{2,1,0:T(2,128)} %param.3) | copy-start | bytes 147460
  393.8 191.1 %all-reduce.3.cloned.1.call-start = ((), (), s32[]{:S(2)}) async-start(), calls=%async_computation.3 | async-start | bytes 2097152 | tf_op jit(solution)/shard_map/psum | solution.py:36
Sparse Core Ops, SparseCore 0:
  11.3 81.1 all-gather.1
  393.9 139.6 reduce-scatter.1
  536.6 48.2 all-reduce.2
where the time goes:
time: 595 us; the launch traced here: 594 us
  blocking collectives  248 us (42%)
  waiting for transfers between devices  233 us (39%)
  matrix products  52.2 us (9%)
  local copies, waits for them, and re-layouts  26.8 us (5%)
  other arithmetic  19.7 us (3%)
  between operations  13.8 us (2%)
    psum x1, blocking collectives, per_device(): totals, masses = lax.psum((local_totals, local_masses), 'proto')  248 us
    reduce_scatter x1, waiting for transfers between devices, per_device(): lax.psum_scatter(jnp.einsum('bjk,kd->bjd', gradient, cluster_center, prec...  126 us
    all_gather x1, waiting for transfers between devices, per_device(): collected_rows = lax.all_gather(unit, 'proto', axis=0, tiled=True)  57.1 us
    psum x1, waiting for transfers between devices, per_device(): proto_grad = lax.psum(partial_grad, 'view')  49.6 us
    unnamed x13, local copies, waits for them, and re-layouts  26.7 us
    dot_general x1, matrix products, per_device(): jnp.einsum('bjk,kd->bjd', gradient, cluster_center, precision=largest_logit)  23.3 us
    dot_general x1, matrix products, per_device(): jnp.einsum('vhf,xf->vhx', collected_rows, cluster_center, precision=large...  15 us
    dot_general x1, matrix products, per_device(): jnp.einsum('bjk,bjd->kd', gradient, collected_rows, precision=largest_logit)  13.9 us
  transfers between devices with their start and end apart: 3, of which 3 were waited for; matrix products, arithmetic and copies ran while one was open for 7% of the time, Pallas kernels for 0%

commit v1 on v0

v1 whole, which is shorter than its diff:
```python
import jax
import jax.numpy as jnp
from jax import lax
from jax.experimental import pallas as pl
from jax.experimental.pallas import tpu as pltpu
from jax.sharding import PartitionSpec as P

MESH = pl.DeviceIdType.MESH
F32 = jnp.float32
BF16 = jnp.bfloat16
WEIGHT = 4096.0 / 0.1
FIXED_POINT = 2.0 ** (-24)
SCORE_SCALE = 10.0 * 1.4426950408889634

D = 256
KL = 1024
BLK = 48
CH = 4 * BLK
NC = 16
ROWS = NC * CH
ZN, XN = 8, 4

ORDER = [
    ("A", 0), ("A", -1),
    ("A", 1), ("A", 2),
    ("A", -2), ("B", 0, 0),
    ("B", 0, 1), ("A", 3),
    ("A", -3), ("B", -1, 0),
    ("B", 1, 1), ("A", 4),
    ("B", -1, 1), ("B", 1, 0),
    ("B", 2, 0), ("B", 2, 1),
]
POS = {name: at for at, name in enumerate(ORDER)}
BACK = [
    ("B", 2, 0), ("B", 2, 1),
    ("A", 4), ("A", -3),
    ("A", 3), ("B", -1, 0),
    ("B", 1, 1), ("B", -1, 1),
    ("B", 1, 0), ("A", -2),
    ("A", 2), ("A", -1),
    ("A", 1), ("B", 0, 0),
    ("B", 0, 1), ("A", 0),
]
SIB = {}
for _kind in "AB":
    for _at, _name in enumerate([n for n in BACK if n[0] == _kind]):
        SIB[_name] = _at

_NAMES = (
    ["cnt", "pro", "x0", "x1", "x2", "a0"]
    + ["al%d" % t for t in range(1, 5)] + ["ar%d" % t for t in range(1, 5)]
    + ["bl%d" % t for t in range(1, 5)] + ["br%d" % t for t in range(1, 5)]
    + ["b%d" % t for t in range(8)]
    + ["s%d" % t for t in range(8)]
    + ["L%d" % t for t in range(4)] + ["R%d" % t for t in range(4)]
    + ["ZL%d" % t for t in range(4)] + ["ZR%d" % t for t in range(4)]
    + ["XS%d" % t for t in range(3)]
    + ["XL0", "XR0", "XL1a", "XL1b", "XR1a", "XR1b"]
    + ["y%d_%d_%d" % (s, k, h) for s in range(4) for k in range(4) for h in range(2)]
    + ["out%d" % s for s in range(4)]
)
RS = {name: at for at, name in enumerate(_NAMES)}


def wrap(v, n):
    return lax.rem(v + n, n)


def select(i, values):
    out = (i == 0).astype(jnp.int32) * values[0]
    for at in range(1, len(values)):
        out = out + (i == at).astype(jnp.int32) * values[at]
    return out


def split(v):
    hi = v.astype(BF16)
    return hi, (v - hi.astype(F32)).astype(BF16)


def view(ref, index):
    return lambda: ref.at[index]


def dot(a, b):
    return jnp.dot(a, b, preferred_element_type=F32)


def kernel(
    feat, proto, counts, fg, pg_out,
    cnt, u, ut, e, ghi, glo, ug, sib, cth, ctl, chi, clo, pg, pgo, sb, own,
    tbuf, t1, t2, t3, ringl, ringr, xs, xb, zl, zr, y1, y2,
    ssem, rsem, t1s, t2s, t3s, t1r, t2r, t3r,
):
    p = lax.axis_index("proto")
    y = lax.axis_index("view")
    c = lax.rem(p, 2)
    x = lax.rem(p // 2, XN)
    z = p // (2 * XN)

    def dev(zz, xx, cc):
        return {"proto": (zz * XN + xx) * 2 + cc}

    sibling = dev(z, x, 1 - c)
    right_z, left_z = dev(wrap(z + 1, ZN), x, c), dev(wrap(z - 1, ZN), x, c)
    right_x, left_x = dev(z, wrap(x + 1, XN), c), dev(z, wrap(x - 1, XN), c)
    far_x = dev(z, wrap(x + 2, XN), c)
    y0, yb1 = lax.rem(y, 2), y // 2
    mate_a = {"view": yb1 * 2 + (1 - y0)}
    mate_b = {"view": (1 - yb1) * 2 + (1 - y0)}
    fbit, gbit = lax.rem(y0 + yb1, 2), yb1

    g8 = lax.rem(p, 8)
    peers = [dict(proto=z * 8 + lax.rem(g8 + k, 8)) for k in range(1, 8)]
    ranks = [lax.rem(g8 + k, 8) for k in range(1, 8)]
    zpeers = [dev(lax.rem(z + k, ZN), x, c) for k in range(1, 8)]

    cnt_copy = pltpu.make_async_copy(counts, cnt, rsem.at[RS["cnt"]])
    cnt_copy.start()
    pro_copy = pltpu.make_async_copy(proto, pg, rsem.at[RS["pro"]])
    pro_copy.start()

    barrier = pltpu.get_barrier_semaphore()
    for d in peers + zpeers + [mate_a, mate_b]:
        pl.semaphore_signal(barrier, inc=1, device_id=d, device_id_type=MESH)

    sent = [[], [], []]

    def send(who, src, dst, name, device):
        at = len(sent[who]) + (0 if who < 2 else 64)

        def make():
            return pltpu.make_async_remote_copy(
                src_ref=src() if callable(src) else src, dst_ref=dst() if callable(dst) else dst,
                send_sem=ssem.at[at], recv_sem=rsem.at[RS[name]],
                device_id=device, device_id_type=MESH,
            )

        sent[who].append(make)
        make().start()

    def arrive(dst, name):
        pltpu.make_async_remote_copy(
            src_ref=dst, dst_ref=dst, send_sem=ssem.at[0], recv_sem=rsem.at[RS[name]],
            device_id=sibling, device_id_type=MESH,
        ).wait_recv()

    q_of = {}
    for name in ORDER:
        if name[0] == "A":
            q_of[name] = wrap(z + name[1], ZN)
        else:
            q_of[name] = 8 + wrap(x + name[1], XN) * 2 + name[2]
    at_of = {name: pl.multiple_of(q * CH, CH) for name, q in q_of.items()}

    def urows(name, lo=0, n=CH):
        return u.at[pl.ds(pl.multiple_of(at_of[name] + lo, 8), n)]

    def ublk(dz):
        return u.at[pl.ds(pl.multiple_of(ROWS // 2 + x * 2 * CH + wrap(z + dz, ZN) * BLK, 8), BLK)]

    def ublk_half(dz, h):
        at = ROWS // 2 + x * 2 * CH + wrap(z + dz, ZN) * BLK + h * (BLK // 2)
        return u.at[pl.ds(pl.multiple_of(at, 8), BLK // 2)]

    def ublk_a(dx):
        return u.at[pl.ds(pl.multiple_of(z * CH + wrap(x + dx, XN) * BLK, 8), BLK)]

    own_at = pl.multiple_of(
        jnp.where(c == 0, z * CH + x * BLK, ROWS // 2 + x * 2 * CH + z * BLK), 8
    )
    own_a, blocks_a = ublk_a(0), [ublk_a(-1), ublk_a(1), ublk_a(2)]
    blk = {d: ublk(d) for d in range(-3, 4)}
    half4 = [ublk_half(4, 0), ublk_half(4, 1)]
    halfm3, halfp3 = ublk_half(-3, 0), ublk_half(3, 1)
    rows = {name: urows(name) for name in ORDER}
    a4h = [urows(("A", 4), 0, CH // 2), urows(("A", 4), CH // 2, CH // 2)]
    am3h, ap3h = urows(("A", -3), 0, CH // 2), urows(("A", 3), CH // 2, CH // 2)

    def load_features():
        crops = []
        for j in range(2):
            crops.append(jnp.concatenate([feat[pl.ds(kt * 2 + j, BLK // 2, stride=4), :] for kt in range(2)], axis=1))
        f = jnp.concatenate(crops, axis=0)
        norm = jnp.sqrt(jnp.sum(f * f, axis=1, keepdims=True) + 1e-6)
        return f, norm

    f, norm = load_features()
    u[pl.ds(own_at, BLK), :] = f / norm

    pl.semaphore_wait(barrier, 16)

    @pl.when(c == 0)
    def _():
        send(0, own_a, own_a, "x0", right_x)
        send(0, own_a, own_a, "x1", left_x)
        send(0, own_a, own_a, "x2", far_x)

    @pl.when(c == 1)
    def _():
        send(1, blk[0], blk[0], "bl1", right_z)
        send(1, blk[0], blk[0], "br1", left_z)

    pro_copy.wait()

    def centroids(i, carry):
        at = pl.multiple_of(i * 256, 256)
        v = pg[pl.ds(at, 256), :]
        v = v / jnp.sqrt(jnp.sum(v * v, axis=1, keepdims=True) + 1e-6)
        hi, lo = split(v)
        chi[pl.ds(at, 256), :] = hi
        clo[pl.ds(at, 256), :] = lo
        hi, lo = split(jnp.transpose(v * SCORE_SCALE))
        cth[:, pl.ds(at, 256)] = hi
        ctl[:, pl.ds(at, 256)] = lo
        return carry

    lax.fori_loop(0, KL // 256, centroids, 0)
    tbuf[...] = jnp.zeros_like(tbuf)
    eye = lax.broadcasted_iota(jnp.int32, (CH // 2, 128), 0) == lax.broadcasted_iota(jnp.int32, (CH // 2, 128), 1)

    def core1_ring(t):
        if t < 4:
            arrive(blk[-t], "bl%d" % t)
            arrive(blk[t], "br%d" % t)
        else:
            arrive(half4[0], "bl4")
            arrive(half4[1], "br4")
        if t < 3:
            send(1, blk[-t], blk[-t], "bl%d" % (t + 1), right_z)
            send(1, blk[t], blk[t], "br%d" % (t + 1), left_z)
        elif t == 3:
            send(1, halfm3, halfm3, "bl4", right_z)
            send(1, halfp3, halfp3, "br4", left_z)

    def stage_a(t):
        if t < 4:
            left, right = rows[("A", -t)], rows[("A", t)]
        else:
            left, right = a4h
        arrive(left, "al%d" % t)
        arrive(right, "ar%d" % t)

        @pl.when(c == 0)
        def _():
            if t < 3:
                send(0, left, left, "al%d" % (t + 1), right_z)
                send(0, right, right, "ar%d" % (t + 1), left_z)
            elif t == 3:
                send(0, am3h, am3h, "al4", right_z)
                send(0, ap3h, ap3h, "ar4", left_z)
            send(0, left, left, "al%d" % t, sibling)
            send(0, right, right, "ar%d" % t, sibling)

    def stage_b(name, at, onward=None):
        arrive(rows[name], "b%d" % at)

        @pl.when(c == 1)
        def _():
            if onward is not None:
                send(1, rows[name], rows[name], "b%d" % onward[0], onward[1])
            send(1, rows[name], rows[name], "b%d" % at, sibling)

    def gather_comm(i):
        if i == 0:
            @pl.when(c == 0)
            def _():
                for k in range(3):
                    arrive(blocks_a[k], "x%d" % k)
                r = rows[("A", 0)]
                send(0, r, r, "al1", right_z)
                send(0, r, r, "ar1", left_z)
                send(0, r, r, "a0", sibling)

            @pl.when(c == 1)
            def _():
                for t in (1, 2, 3):
                    core1_ring(t)
                arrive(rows[("A", 0)], "a0")

            stage_a(1)
        elif i == 1:
            @pl.when(c == 1)
            def _():
                core1_ring(4)
                ra, rb = rows[("B", 0, 0)], rows[("B", 0, 1)]
                send(1, ra, ra, "b2", right_x)
                send(1, rb, rb, "b5", left_x)
                send(1, rb, rb, "b3", right_x)
                send(1, ra, ra, "b4", left_x)
                send(1, ra, ra, "b0", sibling)
                send(1, rb, rb, "b1", sibling)

            stage_a(2)
        elif i == 2:
            @pl.when(c == 0)
            def _():
                arrive(rows[("B", 0, 0)], "b0")
                arrive(rows[("B", 0, 1)], "b1")
        elif i == 3:
            stage_a(3)
        elif i == 4:
            stage_b(("B", -1, 0), 2, (6, right_x))
        elif i == 5:
            stage_b(("B", 1, 1), 5, (7, left_x))
            stage_a(4)
        elif i == 6:
            stage_b(("B", -1, 1), 3)
            stage_b(("B", 1, 0), 4)
        elif i == 7:
            stage_b(("B", 2, 0), 6)
            stage_b(("B", 2, 1), 7)

    def source(q, k):
        over = q - 8
        return jnp.where(q < 8, q * 8 + 2 * k, (lax.rem(over + 8, 2) * 4 + k) * 8 + (over + 8) // 2 * 2 - 8 + 1)

    def counts_at(first, kt):
        return jnp.concatenate(
            [cnt[pl.ds(first + (kt * 2 + 1 - j), BLK // 2, stride=16), :] for j in range(2)], axis=0
        )

    qs = [q_of[name] for name in ORDER]

    def forward(i, carry):
        for k in range(8):
            @pl.when(i == k)
            def _(k=k):
                gather_comm(k)

        q2 = [select(i, qs[h::2]) for h in range(2)]
        v = jnp.concatenate([u[pl.ds(pl.multiple_of(q * CH, 8), CH), :] for q in q2], axis=0)
        hi, lo = split(v)
        at = pl.multiple_of(i * 2 * CH, 2 * CH)
        part = None
        for n in range(4):
            cols = pl.ds(n * 256, 256)
            s = dot(hi, cth[:, cols]) + dot(lo, cth[:, cols]) + dot(hi, ctl[:, cols])
            ex = jnp.exp2(s)
            e[pl.ds(at, 2 * CH), cols] = ex
            two = ex[:, :128] + ex[:, 128:]
            part = two if part is None else part + two
        total = jnp.sum(part, axis=1, keepdims=True)
        hi, lo = split(jnp.transpose(v))
        ut[0:D, pl.ds(at, 2 * CH)] = hi
        ut[D : 2 * D, pl.ds(at, 2 * CH)] = lo
        for h in range(2):
            for k in range(2):
                col = total[h * CH + k * (CH // 2) : h * CH + (k + 1) * (CH // 2)]
                row = jnp.sum(jnp.where(eye, col, 0.0), axis=0, keepdims=True)
                tbuf[q2[h], k : k + 1, :] = row
                masses = []
                for b in range(2):
                    first = source(q2[h], 2 * k + b) * (BLK // 2 * 16)
                    m = counts_at(first, 0)
                    for kt in range(1, 8):
                        m = m + counts_at(first, kt)
                    masses.append(m.astype(F32))
                col = jnp.sum(jnp.concatenate(masses, axis=0), axis=1, keepdims=True)
                row = jnp.sum(jnp.where(eye, col, 0.0), axis=0, keepdims=True)
                tbuf[q2[h], 2 + k : 3 + k, :] = row
        return carry

    cnt_copy.wait()
    lax.fori_loop(0, 8, forward, 0)

    def small(src, dst, ss, rr, device):
        return pltpu.make_async_remote_copy(
            src_ref=src, dst_ref=dst, send_sem=ss, recv_sem=rr, device_id=device, device_id_type=MESH
        )

    def eighth(buf, r):
        return buf.at[pl.ds(pl.multiple_of(r * 2, 2), 2)]

    first = [small(eighth(tbuf, ranks[k]), t1.at[k], t1s.at[k], t1r.at[k], peers[k]) for k in range(7)]
    for copy in first:
        copy.start()
    for copy in first:
        copy.wait()
    mine = tbuf[pl.ds(g8 * 2, 2)]
    for k in range(7):
        mine = mine + t1[k]
    t2[7] = mine
    second = [small(t2.at[7], t2.at[k], t2s.at[k], t2r.at[k], zpeers[k]) for k in range(7)]
    for copy in second:
        copy.start()
    for copy in second:
        copy.wait()
    mine = t2[7]
    for k in range(7):
        mine = mine + t2[k]
    ratio = (mine[:, 2:4, :] * (FIXED_POINT * WEIGHT)) / jnp.maximum(mine[:, 0:2, :], 1e-30)
    t3[pl.ds(g8 * 2, 2), 0:2, :] = ratio
    third = [small(eighth(t3, g8), eighth(t3, g8), t3s.at[k], t3r.at[k], peers[k]) for k in range(7)]
    for copy in third:
        copy.start()
    for k in range(7):
        small(eighth(t3, ranks[6 - k]), eighth(t3, ranks[6 - k]), t3s.at[k], t3r.at[k], peers[k]).wait_recv()
    for copy in third:
        copy.wait_send()

    def spread(pos, carry):
        q = select(pos, qs)
        for k in range(2):
            row = t3[q, k : k + 1, :]
            col = jnp.sum(jnp.where(eye, row, 0.0), axis=1, keepdims=True)
            at = pl.multiple_of(pos * CH + k * (CH // 2), 8)
            sb[pl.ds(at, CH // 2), :] = jnp.broadcast_to(col, (CH // 2, 128))
        return carry

    lax.fori_loop(0, NC, spread, 0)

    def ypart(s):
        h1, h2 = s * 256, s * 256 + 128

        def ds(at, n):
            return pl.ds(pl.multiple_of(at, 8), n)

        return dict(
            away1=(ds(h1 + (1 - fbit) * 64, 64), ds(h2 + (1 - gbit) * 64, 64)),
            keep1=(ds(h1 + fbit * 64, 64), ds(h2 + gbit * 64, 64)),
            away2=(ds(h1 + fbit * 64 + (1 - gbit) * 32, 32), ds(h2 + gbit * 64 + (1 - fbit) * 32, 32)),
            keep2=(ds(h1 + fbit * 64 + gbit * 32, 32), ds(h2 + gbit * 64 + fbit * 32, 32)),
        )

    yparts = [ypart(s) for s in range(4)]

    def out_copy(s):
        rng = pl.ds(s * 256, 256)
        return pltpu.make_async_copy(pgo.at[rng], pg_out.at[rng], rsem.at[RS["out%d" % s]])

    def ystep(k, s):
        part = yparts[s]
        for h in range(2):
            near, far = (mate_a, mate_b) if h == 0 else (mate_b, mate_a)
            name = "y%d_%d_%d" % (s, k - 1, h)
            prev = "y%d_%d_%d" % (s, k - 2, h)
            if k == 1:
                send(2, view(pg, (part["away1"][h],)), view(y1, (s, h,)), name, near)
            elif k == 2:
                arrive(y1.at[s, h], prev)
                keep = part["keep1"][h]
                pg[keep, :] = pg[keep, :] + y1[s, h]
                send(2, view(pg, (part["away2"][h],)), view(y2, (s, h,)), name, far)
            elif k == 3:
                arrive(y2.at[s, h], prev)
                keep = part["keep2"][h]
                pgo[keep, :] = pg[keep, :] + y2[s, h]
                send(2, view(pgo, (keep,)), view(pgo, (keep,)), name, far)
            elif k == 4:
                arrive(pgo.at[part["away2"][h]], prev)
                send(2, view(pgo, (part["keep1"][h],)), view(pgo, (part["keep1"][h],)), name, near)
            elif k == 5:
                arrive(pgo.at[part["away1"][h]], prev)
        if k == 5:
            out_copy(s).start()

    def slab(s, carry):
        col = pl.multiple_of(s * 256, 256)

        def gradient(pos, carry):
            q = select(pos, qs)
            for k in range(4):
                first = source(q, k) * (BLK // 2 * 16) + s * 4
                at = pl.ds(pl.multiple_of(pos * CH + k * BLK, 16), BLK)
                w = sb[at, :]
                for kt in range(2):
                    cols = pl.ds(pl.multiple_of(col + kt * 128, 128), 128)
                    g = w * e[at, cols] - counts_at(first, kt).astype(F32) * (FIXED_POINT * WEIGHT)
                    hi, lo = split(g)
                    ghi[at, cols] = hi
                    glo[at, cols] = lo
            return carry

        lax.fori_loop(0, NC, gradient, 0)
        cols = pl.ds(col, 256)
        both = dot(ut[...], ghi[:, cols])
        acc = both[:D] + both[D:] + dot(ut[0:D, :], glo[:, cols])
        pg[cols, :] = jnp.transpose(acc)
        for k in range(4):
            @pl.when(s == k)
            def _(k=k):
                for t in range(k + 1):
                    ystep(t + 1, k - t)
        return carry

    lax.fori_loop(0, 4, slab, 0)

    def grows(name, lo=0, n=CH):
        return pl.ds(POS[name] * CH + lo, n)

    def add(dst, buf, src):
        ug[dst, :] = ug[dst, :] + buf[src, :]

    def to_sibling(names):
        for kind in "AB":
            mine = [n for n in names if n[0] == kind]
            if not mine:
                continue
            who = 1 if kind == "A" else 0

            @pl.when(c == who)
            def _():
                for n in mine:
                    send(who, view(ug, (grows(n),)), view(sib, (SIB[n],)), "s%d" % SIB[n], sibling)

    def from_sibling(name):
        arrive(sib.at[SIB[name]], "s%d" % SIB[name])
        ug[grows(name), :] = ug[grows(name), :] + sib[SIB[name]]

    half = CH // 2
    ring_at = [(0, half), (half, CH), (half + CH, CH), (half + 2 * CH, CH)]

    def core0_stage(d):
        if d == 4:
            from_sibling(("A", 4))
            rng = pl.ds(0, half)
            send(0, view(ug, (grows(("A", 4), 0, half),)), view(ringl, (rng,)), "L0", left_z)
            send(0, view(ug, (grows(("A", 4), half, half),)), view(ringr, (rng,)), "R0", right_z)
            return
        lo, n = ring_at[3 - d]
        src, nxt = pl.ds(lo, n), pl.ds(*ring_at[4 - d])
        for sign, buf, tag, to in ((-1, ringl, "L", left_z), (1, ringr, "R", right_z)):
            name = ("A", sign * d)
            from_sibling(name)
            arrive(buf.at[src], "%s%d" % (tag, 3 - d))
            off = half if (d == 3 and sign == 1) else 0
            add(grows(name, off, n), buf, src)
            send(0, view(ug, (grows(name),)), view(buf, (nxt,)), "%s%d" % (tag, 4 - d), to)

    def core0_last():
        from_sibling(("A", 0))
        src = pl.ds(*ring_at[3])
        arrive(ringl.at[src], "L3")
        add(grows(("A", 0)), ringl, src)
        arrive(ringr.at[src], "R3")
        add(grows(("A", 0)), ringr, src)

    base_a = POS[("A", 0)] * CH
    xblock = [pl.ds(pl.multiple_of(base_a + wrap(x + dx, XN) * BLK, 8), BLK) for dx in range(4)]
    xdev = [dev(z, wrap(x + dx, XN), c) for dx in range(4)]

    def core0_x():
        for dx in (1, 2, 3):
            send(0, view(ug, (xblock[dx],)), view(xs, (dx - 1,)), "XS%d" % (dx - 1), xdev[dx])

    def core0_end():
        total = ug[xblock[0], :]
        for dx in (1, 2, 3):
            arrive(xs.at[dx - 1], "XS%d" % (dx - 1))
            total = total + xs[dx - 1]
        own[...] = total

    xbr = [pl.ds(k * CH, CH) for k in range(6)]

    def core1_first():
        from_sibling(("B", 2, 0))
        send(1, view(ug, (grows(("B", 2, 0)),)), view(xb, (xbr[0],)), "XL0", left_x)
        from_sibling(("B", 2, 1))
        send(1, view(ug, (grows(("B", 2, 1)),)), view(xb, (xbr[1],)), "XR0", right_x)

    def core1_near():
        for name, src, tag, dst, out, to in (
            (("B", -1, 0), 0, "XL0", 2, "XL1a", left_x),
            (("B", 1, 1), 1, "XR0", 4, "XR1b", right_x),
        ):
            from_sibling(name)
            arrive(xb.at[xbr[src]], tag)
            add(grows(name), xb, xbr[src])
            send(1, view(ug, (grows(name),)), view(xb, (xbr[dst],)), out, to)

    def core1_near2():
        for name, dst, out, to in (
            (("B", -1, 1), 3, "XL1b", left_x),
            (("B", 1, 0), 5, "XR1a", right_x),
        ):
            from_sibling(name)
            send(1, view(ug, (grows(name),)), view(xb, (xbr[dst],)), out, to)

    def core1_own():
        for name, pair in ((("B", 0, 0), ((2, "XL1a"), (5, "XR1a"))), (("B", 0, 1), ((3, "XL1b"), (4, "XR1b")))):
            from_sibling(name)
            for src, tag in pair:
                arrive(xb.at[xbr[src]], tag)
                add(grows(name), xb, xbr[src])

    base_b = POS[("B", 0, 0)] * CH

    def gblk(dz, lo=0, n=BLK):
        return pl.ds(pl.multiple_of(base_b + wrap(z + dz, ZN) * BLK + lo, 8), n)

    gb = {d: gblk(d) for d in range(-3, 4)}
    hb = BLK // 2
    gh = {(4, 0): gblk(4, 0, hb), (4, 1): gblk(4, hb, hb), (-3, 0): gblk(-3, 0, hb), (3, 1): gblk(3, hb, hb)}
    zat = [pl.ds(0, hb), pl.ds(hb, BLK), pl.ds(hb + BLK, BLK), pl.ds(hb + 2 * BLK, BLK)]

    def core1_z(d):
        if d == 4:
            send(1, view(ug, (gh[(4, 0)],)), view(zl, (zat[0],)), "ZL0", left_z)
            send(1, view(ug, (gh[(4, 1)],)), view(zr, (zat[0],)), "ZR0", right_z)
            return
        for sign, buf, tag, to in ((-1, zl, "ZL", left_z), (1, zr, "ZR", right_z)):
            src, nxt = zat[3 - d], zat[4 - d]
            arrive(buf.at[src], "%s%d" % (tag, 3 - d))
            dst = gh[(sign * 3, 0 if sign < 0 else 1)] if d == 3 else gb[sign * d]
            add(dst, buf, src)
            send(1, view(ug, (gb[sign * d],)), view(buf, (nxt,)), "%s%d" % (tag, 4 - d), to)

    def core1_end():
        arrive(zl.at[zat[3]], "ZL3")
        arrive(zr.at[zat[3]], "ZR3")
        own[...] = ug[gb[0], :] + zl[zat[3], :] + zr[zat[3], :]

    def on(who, *steps):
        @pl.when(c == who)
        def _():
            for step in steps:
                step()

    def back_comm(i):
        to_sibling(BACK[2 * i : 2 * i + 2])
        if i == 0:
            ystep(2, 3), ystep(3, 2), ystep(4, 1)
        elif i == 1:
            on(1, core1_first)
            ystep(5, 0)
        elif i == 2:
            on(0, lambda: core0_stage(4))
            ystep(3, 3), ystep(4, 2)
        elif i == 3:
            on(0, lambda: core0_stage(3))
        elif i == 4:
            on(1, core1_near)
            ystep(4, 3), ystep(5, 1)
        elif i == 5:
            on(1, core1_near2)
        elif i == 6:
            on(0, lambda: core0_stage(2))
        elif i == 7:
            on(0, lambda: core0_stage(1))

    back = [POS[name] for name in BACK]

    def backward(i, carry):
        at = [pl.multiple_of(select(i, back[h::2]) * CH, CH) for h in range(2)]
        hi = jnp.concatenate([ghi[pl.ds(a, CH), :] for a in at], axis=0)
        lo = jnp.concatenate([glo[pl.ds(a, CH), :] for a in at], axis=0)
        grad = dot(hi, chi[...]) + dot(hi, clo[...]) + dot(lo, chi[...])
        for h in range(2):
            ug[pl.ds(at[h], CH), :] = grad[h * CH : (h + 1) * CH]
        for k in range(8):
            @pl.when(i == k)
            def _(k=k):
                back_comm(k)
        return carry

    lax.fori_loop(0, 8, backward, 0)

    on(0, core0_last, core0_x)
    on(1, core1_own, lambda: core1_z(4), lambda: core1_z(3), lambda: core1_z(2), lambda: core1_z(1))
    on(0, core0_end)
    on(1, core1_end)

    f, norm = load_features()
    unit = f / norm
    grad = own[...]
    inner = jnp.sum(unit * grad, axis=1, keepdims=True)
    out = (grad - unit * inner) / norm
    for j in range(2):
        for kt in range(2):
            piece = out[j * (BLK // 2) : (j + 1) * (BLK // 2), kt * 128 : (kt + 1) * 128]
            fg[pl.ds(kt * 2 + j, BLK // 2, stride=4), :] = piece

    ystep(5, 2)
    ystep(5, 3)
    for who in (0, 1):
        @pl.when(c == who)
        def _(who=who):
            for make in sent[who]:
                make().wait_send()
    for make in sent[2]:
        make().wait_send()
    for s in range(4):
        out_copy(s).wait()


def per_device(features, prototypes, code_counts):
    feat = features.reshape(24, 2, 2, 128).transpose(0, 2, 1, 3).reshape(96, 128)
    counts = code_counts.reshape(1536, 2, 8, 128).transpose(0, 2, 1, 3).reshape(1536 * 16, 128)
    vmem, hbm = pl.BlockSpec(memory_space=pltpu.VMEM), pl.BlockSpec(memory_space=pl.ANY)
    half = CH // 2
    dma = pltpu.SemaphoreType.DMA
    fg, pg = pl.pallas_call(
        kernel,
        out_shape=(jax.ShapeDtypeStruct((96, 128), F32), jax.ShapeDtypeStruct((KL, D), F32)),
        in_specs=[vmem, hbm, hbm],
        out_specs=(vmem, hbm),
        scratch_shapes=[
            pltpu.VMEM((1536 * 16, 128), jnp.int32),
            pltpu.VMEM((ROWS, D), F32),
            pltpu.VMEM((2 * D, ROWS), BF16),
            pltpu.VMEM((ROWS, KL), F32),
            pltpu.VMEM((ROWS, KL), BF16),
            pltpu.VMEM((ROWS, KL), BF16),
            pltpu.VMEM((ROWS, D), F32),
            pltpu.VMEM((8, CH, D), F32),
            pltpu.VMEM((D, KL), BF16),
            pltpu.VMEM((D, KL), BF16),
            pltpu.VMEM((KL, D), BF16),
            pltpu.VMEM((KL, D), BF16),
            pltpu.VMEM((KL, D), F32),
            pltpu.VMEM((KL, D), F32),
            pltpu.VMEM((ROWS, 128), F32),
            pltpu.VMEM((BLK, D), F32),
            pltpu.VMEM((NC, 8, 128), F32),
            pltpu.VMEM((7, 2, 8, 128), F32),
            pltpu.VMEM((8, 2, 8, 128), F32),
            pltpu.VMEM((NC, 8, 128), F32),
            pltpu.VMEM((half + 3 * CH, D), F32),
            pltpu.VMEM((half + 3 * CH, D), F32),
            pltpu.VMEM((3, BLK, D), F32),
            pltpu.VMEM((6 * CH, D), F32),
            pltpu.VMEM((BLK // 2 + 3 * BLK, D), F32),
            pltpu.VMEM((BLK // 2 + 3 * BLK, D), F32),
            pltpu.VMEM((4, 2, 64, D), F32),
            pltpu.VMEM((4, 2, 32, D), F32),
            dma((96,)),
            dma((len(RS),)),
            dma((7,)), dma((7,)), dma((7,)), dma((7,)), dma((7,)), dma((7,)),
        ],
        compiler_params=pltpu.CompilerParams(
            collective_id=0, has_side_effects=True, vmem_limit_bytes=60 << 20
        ),
        cost_estimate=pl.CostEstimate(flops=18 * ROWS * KL * D, bytes_accessed=16 << 20, transcendentals=ROWS * KL),
    )(feat, prototypes, counts)
    features_grad = fg.reshape(24, 2, 2, 128).transpose(0, 2, 1, 3).reshape(24, 2, 256)
    return features_grad, pg


def solution(mesh):
    in_specs = (P(("view", "proto"), None, None), P("proto", None), P("view", None, "proto"))
    out_specs = (P(("view", "proto"), None, None), P("proto", None))
    return jax.shard_map(
        per_device, mesh=mesh, in_specs=in_specs, out_specs=out_specs, check_vma=False
    )
```

time: 595 us -> 113 us (0.19)
  blocking collectives: 248 us -> 0 us
  waiting for transfers between devices: 233 us -> 0 us
  Pallas kernels: 0 us -> 108 us
  matrix products: 52.2 us -> 0 us
  local copies, waits for them, and re-layouts: 26.8 us -> 3.68 us
  other arithmetic: 19.7 us -> 0 us
  between operations: 13.8 us -> 0.64 us
    psum x1 -> x0, blocking collectives: 248 us -> none  [per_device(): totals, masses = lax.psum((local_totals, local_masses), 'proto')]
    reduce_scatter x1 -> x0, waiting for transfers between devices: 126 us -> none  [per_device(): lax.psum_scatter(jnp.einsum('bjk,kd->bjd', gradient, cluster_center, prec...]
    pallas_call x0 -> x1, Pallas kernels: none -> 108 us  [per_device(): pl.pallas_call(kernel, out_shape=(jax.ShapeDtypeStruct((96, 128), F32), j...]
    all_gather x1 -> x0, waiting for transfers between devices: 57.1 us -> none  [per_device(): collected_rows = lax.all_gather(unit, 'proto', axis=0, tiled=True)]
    dot_general x3 -> x0, matrix products: 52.2 us -> none  [the longest x1 23.3 us: per_device(): jnp.einsum('bjk,kd->bjd', gradient, cluster_center, precision=largest_logit)]
    psum x1 -> x0, waiting for transfers between devices: 49.6 us -> none  [per_device(): proto_grad = lax.psum(partial_grad, 'view')]
    unnamed x13 -> x2, local copies, waits for them, and re-layouts: 26.7 us -> 3.68 us
    mul x2 -> x0, other arithmetic: 11 us -> none  [the longest x1 9.93 us: per_device(): weight_factor * ((masses / totals)[:, :, None] * exponent - swapped)]
  transfers between devices with their start and end apart: 3 -> 0, of which waited for: 3 -> 0; matrix products, arithmetic and copies ran while one was open for 7% -> 0% of each run, Pallas kernels for 0% -> 0%
where the time goes in v1:
time: 113 us
  Pallas kernels  108 us (96%)
  local copies, waits for them, and re-layouts  3.68 us (3%)
    pallas_call x1, Pallas kernels, per_device(): pl.pallas_call(kernel, out_shape=(jax.ShapeDtypeStruct((96, 128), F32), j...  108 us
    unnamed x2, local copies, waits for them, and re-layouts  3.68 us

profile of v1, /device:TPU:8, one launch (start us, length us, event | category | flops | bytes accessed | tf_op | source)
XLA Modules:
  0.0 112.8 jit_solution(6191767493916226009)
XLA Ops:
  0.6 108.5 %shard_map.50 = (f32[96,128]{1,0:T(8,128)}, f32[1024,256]{1,0:T(8,128)}) custom-call(f32[96,128]{1,0:T(8,128)} %bitcast.17, f32[1024,256]{1,0:T(8,128)} %proto.1, s32[24576,128]{1,0:T(8,128)} %bitcast.16), custom_call_target="tpu_custom_call" | custom-call | flops 14495514624 | bytes 16777216 | tf_op jit(solution)/shard_map/pallas_call | solution.py:693
  109.1 1.4 %copy.10 = f32[24,2,256]{2,1,0:T(2,128)} copy(f32[24,2,256]{2,1,0:T(2,128)} %bitcast.15) | data formatting | bytes 98304
  110.5 2.3 %copy.11 = f32[1024,256]{1,0:T(8,128)} copy(f32[1024,256]{1,0:T(8,128)} %get-tuple-element.9) | data formatting | bytes 2097152

commit v2 on v0

v2 whole, which is shorter than its diff:
```python
import jax
import jax.numpy as jnp
from jax import lax
from jax.experimental import pallas as pl
from jax.experimental.pallas import tpu as pltpu
from jax.sharding import PartitionSpec as P

MESH = pl.DeviceIdType.MESH
F32 = jnp.float32
BF16 = jnp.bfloat16
WEIGHT = 4096.0 / 0.1
FIXED_POINT = 2.0 ** (-24)
SCORE_SCALE = 10.0 * 1.4426950408889634

D = 256
KL = 1024
BLK = 48
HALF = 4 * BLK
GRP = 2 * HALF
ROWS = 8 * GRP
ZN, XN = 8, 4

ORDER = [0, 1, 7, 2, 6, 3, 5, 4]
POS = {dz: at for at, dz in enumerate(ORDER)}
BACK = [4, 3, 5, 2, 6, 1, 7, 0]
FAR = [4, 3, 5, 2, 6]

_NAMES = (
    ["pro"]
    + ["px%d" % d for d in range(1, 4)] + ["pz%d" % d for d in range(1, 8)]
    + ["rz%d_%d" % (d, k) for d in (1, 7) for k in range(1, 4)]
    + ["rx%d_%d" % (d, k) for d in range(2, 7) for k in range(1, 4)]
    + ["s%d" % d for d in range(8)] + ["q%d" % d for d in range(8)]
    + ["gx%d_%d" % (d, k) for d in range(2, 7) for k in range(1, 4)]
    + ["gn1", "gn7"] + ["gz%d" % d for d in range(2, 7)] + ["hx%d" % d for d in range(1, 4)]
    + ["y%d_%d_%d" % (s, k, h) for s in range(4) for k in range(4) for h in range(2)]
    + ["out%d" % s for s in range(4)]
)
RS = {name: at for at, name in enumerate(_NAMES)}


def wrap(v, n):
    return lax.rem(v + n, n)


def select(i, values):
    out = (i == 0).astype(jnp.int32) * values[0]
    for at in range(1, len(values)):
        out = out + (i == at).astype(jnp.int32) * values[at]
    return out


def split(v):
    hi = v.astype(BF16)
    return hi, (v - hi.astype(F32)).astype(BF16)


def view(ref, index):
    return lambda: ref.at[index]


def dot(a, b):
    return jnp.dot(a, b, preferred_element_type=F32)


def kernel(
    feat, proto, counts, fg, pg_out,
    cnt, u, ut, utw, ehi, elo, qhi, qlo, ec, ug, sib, cth, ctl, chi, clo, pg, pgo, own,
    tbuf, t1, t2, t3, gxb, gnb, gzb, hxb, y1, y2,
    ssem, rsem, cntsem, t1s, t2s, t3s, t1r, t2r, t3r,
):
    p = lax.axis_index("proto")
    y = lax.axis_index("view")
    c = lax.rem(p, 2)
    x = lax.rem(p // 2, XN)
    z = p // (2 * XN)

    def dev(zz, xx, cc):
        return {"proto": (zz * XN + xx) * 2 + cc}

    sibling = dev(z, x, 1 - c)
    y0, yb1 = lax.rem(y, 2), y // 2
    mate_a = {"view": yb1 * 2 + (1 - y0)}
    mate_b = {"view": (1 - yb1) * 2 + (1 - y0)}
    fbit, gbit = lax.rem(y0 + yb1, 2), yb1

    g8 = lax.rem(p, 8)
    peers = [dict(proto=z * 8 + lax.rem(g8 + k, 8)) for k in range(1, 8)]
    ranks = [lax.rem(g8 + k, 8) for k in range(1, 8)]
    zpeers = [dev(lax.rem(z + k, ZN), x, c) for k in range(1, 8)]
    xpeers = [dev(z, lax.rem(x + k, XN), c) for k in range(1, 4)]

    pro_copy = pltpu.make_async_copy(proto, pg, rsem.at[RS["pro"]])
    pro_copy.start()

    barrier = pltpu.get_barrier_semaphore()
    for d in peers + zpeers + [mate_a, mate_b]:
        pl.semaphore_signal(barrier, inc=1, device_id=d, device_id_type=MESH)

    sent = []

    def send(src, dst, name, device):
        at = len(sent)

        def make():
            return pltpu.make_async_remote_copy(
                src_ref=src() if callable(src) else src, dst_ref=dst() if callable(dst) else dst,
                send_sem=ssem.at[at], recv_sem=rsem.at[RS[name]],
                device_id=device, device_id_type=MESH,
            )

        sent.append(make)
        make().start()

    def arrive(dst, name):
        pltpu.make_async_remote_copy(
            src_ref=dst, dst_ref=dst, send_sem=ssem.at[0], recv_sem=rsem.at[RS[name]],
            device_id=sibling, device_id_type=MESH,
        ).wait_recv()

    zs = [lax.rem(z + d, ZN) for d in range(8)]
    qs = [zs[d] for d in ORDER]

    def ublk(dz, dx):
        return u.at[pl.ds(pl.multiple_of(zs[dz] * GRP + c * HALF + lax.rem(x + dx, XN) * BLK, 8), BLK)]

    def uhalf(dz, core):
        return u.at[pl.ds(pl.multiple_of(zs[dz] * GRP + core * HALF, 8), HALF)]

    blk = {(dz, dx): ublk(dz, dx) for dz in range(8) for dx in range(4)}
    mine_of = [uhalf(dz, c) for dz in range(8)]
    theirs_of = [uhalf(dz, 1 - c) for dz in range(8)]
    own_at = pl.multiple_of(zs[0] * GRP + c * HALF + x * BLK, 8)
    vb = BLK // 2 * 16

    def count_copies(i):
        slot = lax.rem(i, 3)
        copies = []
        group = select(i, qs)
        for b in range(8):
            owner = group * 8 + (b % 4) * 2 + b // 4
            copies.append(
                pltpu.make_async_copy(
                    counts.at[pl.ds(pl.multiple_of(owner * vb, vb), vb)],
                    cnt.at[slot, pl.ds(b * vb, vb)],
                    cntsem.at[slot],
                )
            )
        return copies

    def fetch(i, carry):
        for copy in count_copies(i):
            copy.start()
        return carry

    lax.fori_loop(0, 2, fetch, 0)

    def load_features():
        crops = []
        for j in range(2):
            crops.append(jnp.concatenate([feat[pl.ds(kt * 2 + j, BLK // 2, stride=4), :] for kt in range(2)], axis=1))
        f = jnp.concatenate(crops, axis=0)
        norm = jnp.sqrt(jnp.sum(f * f, axis=1, keepdims=True) + 1e-6)
        return f, norm

    f, norm = load_features()
    u[pl.ds(own_at, BLK), :] = f / norm

    pl.semaphore_wait(barrier, 16)

    own_blk = blk[0, 0]
    for d in (1, 3, 2):
        send(own_blk, own_blk, "px%d" % d, xpeers[d - 1])
    for d in (4, 3, 5, 2, 6, 1, 7):
        send(own_blk, own_blk, "pz%d" % d, zpeers[d - 1])

    pro_copy.wait()

    def centroids(i, carry):
        at = pl.multiple_of(i * 256, 256)
        v = pg[pl.ds(at, 256), :]
        v = v / jnp.sqrt(jnp.sum(v * v, axis=1, keepdims=True) + 1e-6)
        hi, lo = split(v)
        chi[pl.ds(at, 256), :] = hi
        clo[pl.ds(at, 256), :] = lo
        hi, lo = split(jnp.transpose(v * SCORE_SCALE))
        cth[:, pl.ds(at, 256)] = hi
        ctl[:, pl.ds(at, 256)] = lo
        return carry

    lax.fori_loop(0, KL // 256, centroids, 0)
    tbuf[...] = jnp.zeros_like(tbuf)
    eye = lax.broadcasted_iota(jnp.int32, (128, 128), 0) == lax.broadcasted_iota(jnp.int32, (128, 128), 1)

    def to_rows(col, at, first):
        for k in range(3):
            row = jnp.sum(jnp.where(eye, col[k * 128 : (k + 1) * 128], 0.0), axis=0, keepdims=True)
            tbuf[at, first + k : first + k + 1, :] = row

    def relay_z():
        for d in (1, 2, 3):
            arrive(blk[0, 4 - d], "px%d" % d)
        for d in (1, 2, 3):
            send(blk[0, d], blk[0, d], "rz1_%d" % d, zpeers[0])
            send(blk[0, d], blk[0, d], "rz7_%d" % d, zpeers[6])
        send(mine_of[0], mine_of[0], "s0", sibling)

    def relay_x(dz):
        b = blk[dz, 0]
        arrive(b, "pz%d" % (8 - dz))
        for d in (1, 3, 2):
            send(b, b, "rx%d_%d" % (dz, d), xpeers[d - 1])

    def collect(dz):
        if dz in (1, 7):
            arrive(blk[dz, 0], "pz%d" % (8 - dz))
            for d in (1, 2, 3):
                arrive(blk[dz, d], "rz%d_%d" % (8 - dz, d))
        else:
            for d in (1, 2, 3):
                arrive(blk[dz, 4 - d], "rx%d_%d" % (dz, d))
        send(mine_of[dz], mine_of[dz], "s%d" % dz, sibling)

    def use(dz):
        arrive(theirs_of[dz], "s%d" % dz)

    def early_comm(i):
        if i == 3:
            relay_z()
        elif i == 5:
            relay_x(2), relay_x(6)
        elif i == 6:
            relay_x(3), relay_x(5)
        elif i == 7:
            relay_x(4)

    def gather_comm(i):
        if i == 0:
            collect(1), collect(7)
        elif i < 6:
            collect(ORDER[i + 2])
        use(ORDER[i])

    def codes(i, carry):
        for k in range(8):
            @pl.when(i == k)
            def _(k=k):
                early_comm(k)

        slot = lax.rem(i, 3)
        pltpu.make_async_copy(cnt.at[slot], cnt.at[slot], cntsem.at[slot]).wait()

        @pl.when(i < 6)
        def _():
            fetch(i + 2, 0)

        at = pl.multiple_of(i * GRP, GRP)
        sums = []
        for b in range(8):
            rng = pl.ds(pl.multiple_of(at + b * BLK, 16), BLK)
            mass = None
            for kt in range(8):
                v = jnp.concatenate(
                    [cnt[slot, pl.ds(b * vb + kt * 2 + 1 - j, BLK // 2, stride=16), :] for j in range(2)], axis=0
                ).astype(F32)
                mass = v if mass is None else mass + v
                hi, lo = split(v)
                cols = pl.ds(kt * 128, 128)
                qhi[rng, cols] = hi
                qlo[rng, cols] = lo
            sums.append(mass)
        to_rows(jnp.sum(jnp.concatenate(sums, axis=0), axis=1, keepdims=True), select(i, qs), 3)
        rng = pl.ds(at, GRP)
        hi, lo = qhi[rng, :], qlo[rng, :]
        ug[rng, :] = dot(hi, chi[...]) + dot(hi, clo[...]) + dot(lo, chi[...])
        return carry

    def forward(i, carry):
        for k in range(8):
            @pl.when(i == k)
            def _(k=k):
                gather_comm(k)

        group = select(i, qs)
        v = u[pl.ds(pl.multiple_of(group * GRP, 8), GRP), :]
        hi, lo = split(v)
        at = pl.multiple_of(i * GRP, GRP)
        part = None
        for n in range(4):
            cols = pl.ds(n * 256, 256)
            s = dot(hi, cth[:, cols]) + dot(lo, cth[:, cols]) + dot(hi, ctl[:, cols])
            ex = jnp.exp2(s)
            hi_e, lo_e = split(ex)
            ehi[pl.ds(at, GRP), cols] = hi_e
            elo[pl.ds(at, GRP), cols] = lo_e
            two = ex[:, :128] + ex[:, 128:]
            part = two if part is None else part + two
        total = jnp.sum(part, axis=1, keepdims=True)
        hi, lo = split(jnp.transpose(v))
        ut[0:D, pl.ds(at, GRP)] = hi
        ut[D : 2 * D, pl.ds(at, GRP)] = lo
        to_rows(total, group, 0)
        return carry

    lax.fori_loop(0, 8, codes, 0)
    lax.fori_loop(0, 8, forward, 0)

    def small(src, dst, ss, rr, device):
        return pltpu.make_async_remote_copy(
            src_ref=src, dst_ref=dst, send_sem=ss, recv_sem=rr, device_id=device, device_id_type=MESH
        )

    def codes_slab(s):
        cols = pl.ds(s * 256, 256)
        both = dot(ut[...], qhi[:, cols])
        acc = both[:D] + both[D:] + dot(ut[0:D, :], qlo[:, cols])
        pg[cols, :] = jnp.transpose(acc) * (-FIXED_POINT * WEIGHT)

    def forward_grad(i, carry):
        rng = pl.ds(pl.multiple_of(i * GRP, GRP), GRP)
        hi, lo = ehi[rng, :], elo[rng, :]
        ec[rng, :] = dot(hi, chi[...]) + dot(hi, clo[...]) + dot(lo, chi[...])
        return carry

    first = [small(tbuf.at[ranks[k]], t1.at[k], t1s.at[k], t1r.at[k], peers[k]) for k in range(7)]
    for copy in first:
        copy.start()
    codes_slab(0)
    codes_slab(1)
    for copy in first:
        copy.wait()
    mine = tbuf[g8]
    for k in range(7):
        mine = mine + t1[k]
    t2[7] = mine
    second = [small(t2.at[7], t2.at[k], t2s.at[k], t2r.at[k], zpeers[k]) for k in range(7)]
    for copy in second:
        copy.start()
    codes_slab(2)
    codes_slab(3)
    lax.fori_loop(0, 2, forward_grad, 0)
    for copy in second:
        copy.wait()
    mine = t2[7]
    for k in range(7):
        mine = mine + t2[k]
    t3[g8, 0:3, :] = mine[3:6, :] * (FIXED_POINT * WEIGHT) / mine[0:3, :]
    third = [small(t3.at[g8], t3.at[g8], t3s.at[k], t3r.at[k], peers[k]) for k in range(7)]
    for copy in third:
        copy.start()
    lax.fori_loop(2, 8, forward_grad, 0)
    for k in range(7):
        small(t3.at[ranks[6 - k]], t3.at[ranks[6 - k]], t3s.at[k], t3r.at[k], peers[k]).wait_recv()
    for copy in third:
        copy.wait_send()

    def ypart(s):
        h1, h2 = s * 256, s * 256 + 128

        def ds(at, n):
            return pl.ds(pl.multiple_of(at, 8), n)

        return dict(
            away1=(ds(h1 + (1 - fbit) * 64, 64), ds(h2 + (1 - gbit) * 64, 64)),
            keep1=(ds(h1 + fbit * 64, 64), ds(h2 + gbit * 64, 64)),
            away2=(ds(h1 + fbit * 64 + (1 - gbit) * 32, 32), ds(h2 + gbit * 64 + (1 - fbit) * 32, 32)),
            keep2=(ds(h1 + fbit * 64 + gbit * 32, 32), ds(h2 + gbit * 64 + fbit * 32, 32)),
        )

    yparts = [ypart(s) for s in range(4)]

    def out_copy(s):
        rng = pl.ds(s * 256, 256)
        return pltpu.make_async_copy(pgo.at[rng], pg_out.at[rng], rsem.at[RS["out%d" % s]])

    def ystep(k, s):
        part = yparts[s]
        for h in range(2):
            near, far = (mate_a, mate_b) if h == 0 else (mate_b, mate_a)
            name = "y%d_%d_%d" % (s, k - 1, h)
            prev = "y%d_%d_%d" % (s, k - 2, h)
            if k == 1:
                send(view(pg, (part["away1"][h],)), view(y1, (s, h,)), name, near)
            elif k == 2:
                arrive(y1.at[s, h], prev)
                keep = part["keep1"][h]
                pg[keep, :] = pg[keep, :] + y1[s, h]
                send(view(pg, (part["away2"][h],)), view(y2, (s, h,)), name, far)
            elif k == 3:
                arrive(y2.at[s, h], prev)
                keep = part["keep2"][h]
                pgo[keep, :] = pg[keep, :] + y2[s, h]
                send(view(pgo, (keep,)), view(pgo, (keep,)), name, far)
            elif k == 4:
                arrive(pgo.at[part["away2"][h]], prev)
                send(view(pgo, (part["keep1"][h],)), view(pgo, (part["keep1"][h],)), name, near)
            elif k == 5:
                arrive(pgo.at[part["away1"][h]], prev)
        if k == 5:
            out_copy(s).start()

    def slab(s, carry):
        col = pl.multiple_of(s * 256, 256)

        cols = pl.ds(col, 256)
        both = dot(utw[...], ehi[:, cols])
        acc = both[:D] + both[D:] + dot(utw[0:D, :], elo[:, cols])
        pg[cols, :] = jnp.transpose(acc) + pg[cols, :]
        for k in range(4):
            @pl.when(s == k)
            def _(k=k):
                slab_comm(k)
        return carry

    mine_at = [pl.ds(pl.multiple_of(POS[dz] * GRP + c * HALF, 8), HALF) for dz in range(8)]
    theirs_at = [pl.ds(pl.multiple_of(POS[dz] * GRP + (1 - c) * HALF, 8), HALF) for dz in range(8)]

    def gblk(dz, dx):
        return pl.ds(pl.multiple_of(POS[dz] * GRP + c * HALF + lax.rem(x + dx, XN) * BLK, 8), BLK)

    gb = {(dz, dx): gblk(dz, dx) for dz in range(8) for dx in range(4)}

    def from_sibling(dz):
        arrive(sib.at[dz], "q%d" % dz)
        ug[mine_at[dz], :] = ug[mine_at[dz], :] + sib[dz]

    def sums_out(dz):
        from_sibling(dz)
        if dz in (1, 7):
            send(view(ug, (mine_at[dz],)), view(gnb, (dz // 7,)), "gn%d" % dz, zpeers[dz - 1])
        else:
            for d in (2, 1, 3):
                send(view(ug, (gb[dz, d],)), view(gxb, ((dz - 2) * 3 + d - 1,)), "gx%d_%d" % (dz, d), xpeers[d - 1])

    def sums_onward(dz):
        total = ug[gb[dz, 0], :]
        for d in (1, 2, 3):
            arrive(gxb.at[(dz - 2) * 3 + d - 1], "gx%d_%d" % (dz, d))
            total = total + gxb[(dz - 2) * 3 + d - 1]
        ug[gb[dz, 0], :] = total
        send(view(ug, (gb[dz, 0],)), view(gzb, (dz - 2,)), "gz%d" % dz, zpeers[dz - 1])

    def sums_here():
        from_sibling(0)
        for k, dz in enumerate((1, 7)):
            arrive(gnb.at[k], "gn%d" % dz)
        ug[mine_at[0], :] = ug[mine_at[0], :] + gnb[0] + gnb[1]
        for d in (2, 1, 3):
            send(view(ug, (gb[0, d],)), view(hxb, (d - 1,)), "hx%d" % d, xpeers[d - 1])

    def sums_end():
        total = ug[gb[0, 0], :]
        for d in (1, 2, 3):
            arrive(hxb.at[d - 1], "hx%d" % d)
            total = total + hxb[d - 1]
        for d in (2, 6, 3, 5, 4):
            arrive(gzb.at[d - 2], "gz%d" % d)
            total = total + gzb[d - 2]
        own[...] = total

    def slab_comm(k):
        ystep(1, k)
        if k == 0:
            for dz in BACK[:7]:
                sums_out(dz)
        else:
            if k >= 2:
                ystep(2, k - 2)

    def column(group):
        cols = []
        for k in range(3):
            cols.append(jnp.sum(jnp.where(eye, t3[group, k : k + 1, :], 0.0), axis=1, keepdims=True))
        return jnp.concatenate(cols, axis=0)

    def backward(i, carry):
        rng = pl.ds(pl.multiple_of(select(i, back) * GRP, GRP), GRP)
        w = jnp.broadcast_to(column(select(i, backq)), (GRP, D))
        ug[rng, :] = w * ec[rng, :] - ug[rng, :] * (FIXED_POINT * WEIGHT)
        for k in range(8):
            @pl.when(i == k)
            def _(k=k):
                dz = BACK[k]
                send(view(ug, (theirs_at[dz],)), view(sib, (dz,)), "q%d" % dz, sibling)
        return carry

    def weighted(i, carry):
        group = select(i, qs)
        for k in range(3):
            cols = pl.ds(pl.multiple_of(i * GRP + k * 128, 128), 128)
            v = (ut[0:D, cols].astype(F32) + ut[D : 2 * D, cols].astype(F32)) * t3[group, k : k + 1, :]
            hi, lo = split(v)
            utw[0:D, cols] = hi
            utw[D : 2 * D, cols] = lo
        return carry

    back = [POS[dz] for dz in BACK]
    backq = [zs[dz] for dz in BACK]
    lax.fori_loop(0, 8, backward, 0)
    lax.fori_loop(0, 8, weighted, 0)
    lax.fori_loop(0, 4, slab, 0)

    ystep(2, 2)
    ystep(3, 0)
    sums_here()
    ystep(2, 3)
    ystep(3, 1)
    for dz in FAR:
        sums_onward(dz)
    ystep(3, 2)
    ystep(4, 0)
    ystep(3, 3)
    ystep(4, 1)
    ystep(4, 2)
    ystep(5, 0)
    sums_end()

    f, norm = load_features()
    unit = f / norm
    grad = own[...]
    inner = jnp.sum(unit * grad, axis=1, keepdims=True)
    out = (grad - unit * inner) / norm
    for j in range(2):
        for kt in range(2):
            piece = out[j * (BLK // 2) : (j + 1) * (BLK // 2), kt * 128 : (kt + 1) * 128]
            fg[pl.ds(kt * 2 + j, BLK // 2, stride=4), :] = piece

    ystep(4, 3)
    ystep(5, 1)
    ystep(5, 2)
    ystep(5, 3)
    for make in sent:
        make().wait_send()
    for s in range(4):
        out_copy(s).wait()


def per_device(features, prototypes, code_counts):
    feat = features.reshape(24, 2, 2, 128).transpose(0, 2, 1, 3).reshape(96, 128)
    counts = code_counts.reshape(1536, 2, 8, 128).transpose(0, 2, 1, 3).reshape(1536 * 16, 128)
    vmem, hbm = pl.BlockSpec(memory_space=pltpu.VMEM), pl.BlockSpec(memory_space=pl.ANY)
    dma = pltpu.SemaphoreType.DMA
    fg, pg = pl.pallas_call(
        kernel,
        out_shape=(jax.ShapeDtypeStruct((96, 128), F32), jax.ShapeDtypeStruct((KL, D), F32)),
        in_specs=[vmem, hbm, hbm],
        out_specs=(vmem, hbm),
        scratch_shapes=[
            pltpu.VMEM((3, 8 * BLK // 2 * 16, 128), jnp.int32),
            pltpu.VMEM((ROWS, D), F32),
            pltpu.VMEM((2 * D, ROWS), BF16),
            pltpu.VMEM((2 * D, ROWS), BF16),
            pltpu.VMEM((ROWS, KL), BF16),
            pltpu.VMEM((ROWS, KL), BF16),
            pltpu.VMEM((ROWS, KL), BF16),
            pltpu.VMEM((ROWS, KL), BF16),
            pltpu.VMEM((ROWS, D), F32),
            pltpu.VMEM((ROWS, D), F32),
            pltpu.VMEM((8, HALF, D), F32),
            pltpu.VMEM((D, KL), BF16),
            pltpu.VMEM((D, KL), BF16),
            pltpu.VMEM((KL, D), BF16),
            pltpu.VMEM((KL, D), BF16),
            pltpu.VMEM((KL, D), F32),
            pltpu.VMEM((KL, D), F32),
            pltpu.VMEM((BLK, D), F32),
            pltpu.VMEM((8, 8, 128), F32),
            pltpu.VMEM((7, 8, 128), F32),
            pltpu.VMEM((8, 8, 128), F32),
            pltpu.VMEM((8, 8, 128), F32),
            pltpu.VMEM((15, BLK, D), F32),
            pltpu.VMEM((2, HALF, D), F32),
            pltpu.VMEM((5, BLK, D), F32),
            pltpu.VMEM((3, BLK, D), F32),
            pltpu.VMEM((4, 2, 64, D), F32),
            pltpu.VMEM((4, 2, 32, D), F32),
            dma((128,)),
            dma((len(RS),)),
            dma((3,)),
            dma((7,)), dma((7,)), dma((7,)), dma((7,)), dma((7,)), dma((7,)),
        ],
        compiler_params=pltpu.CompilerParams(
            collective_id=0, has_side_effects=True, vmem_limit_bytes=60 << 20
        ),
        cost_estimate=pl.CostEstimate(flops=18 * ROWS * KL * D, bytes_accessed=16 << 20, transcendentals=ROWS * KL),
    )(feat, prototypes, counts)
    features_grad = fg.reshape(24, 2, 2, 128).transpose(0, 2, 1, 3).reshape(24, 2, 256)
    return features_grad, pg


def solution(mesh):
    in_specs = (P(("view", "proto"), None, None), P("proto", None), P("view", None, "proto"))
    out_specs = (P(("view", "proto"), None, None), P("proto", None))
    return jax.shard_map(
        per_device, mesh=mesh, in_specs=in_specs, out_specs=out_specs, check_vma=False
    )
```

time: 595 us -> 84 us (0.14)
  blocking collectives: 248 us -> 0 us
  waiting for transfers between devices: 233 us -> 0 us
  Pallas kernels: 0 us -> 79.3 us
  matrix products: 52.2 us -> 0 us
  local copies, waits for them, and re-layouts: 26.8 us -> 3.68 us
  other arithmetic: 19.7 us -> 0 us
  between operations: 13.8 us -> 0.64 us
    psum x1 -> x0, blocking collectives: 248 us -> none  [per_device(): totals, masses = lax.psum((local_totals, local_masses), 'proto')]
    reduce_scatter x1 -> x0, waiting for transfers between devices: 126 us -> none  [per_device(): lax.psum_scatter(jnp.einsum('bjk,kd->bjd', gradient, cluster_center, prec...]
    pallas_call x0 -> x1, Pallas kernels: none -> 79.3 us  [per_device(): pl.pallas_call(kernel, out_shape=(jax.ShapeDtypeStruct((96, 128), F32), j...]
    all_gather x1 -> x0, waiting for transfers between devices: 57.1 us -> none  [per_device(): collected_rows = lax.all_gather(unit, 'proto', axis=0, tiled=True)]
    dot_general x3 -> x0, matrix products: 52.2 us -> none  [the longest x1 23.3 us: per_device(): jnp.einsum('bjk,kd->bjd', gradient, cluster_center, precision=largest_logit)]
    psum x1 -> x0, waiting for transfers between devices: 49.6 us -> none  [per_device(): proto_grad = lax.psum(partial_grad, 'view')]
    unnamed x13 -> x2, local copies, waits for them, and re-layouts: 26.7 us -> 3.68 us
    mul x2 -> x0, other arithmetic: 11 us -> none  [the longest x1 9.93 us: per_device(): weight_factor * ((masses / totals)[:, :, None] * exponent - swapped)]
  transfers between devices with their start and end apart: 3 -> 0, of which waited for: 3 -> 0; matrix products, arithmetic and copies ran while one was open for 7% -> 0% of each run, Pallas kernels for 0% -> 0%
where the time goes in v2:
time: 84 us; the launch traced here: 83.6 us
  Pallas kernels  79.3 us (94%)
  local copies, waits for them, and re-layouts  3.68 us (4%)
    pallas_call x1, Pallas kernels, per_device(): pl.pallas_call(kernel, out_shape=(jax.ShapeDtypeStruct((96, 128), F32), j...  79.3 us
    unnamed x2, local copies, waits for them, and re-layouts  3.68 us

profile of v2, /device:TPU:8, one launch (start us, length us, event | category | flops | bytes accessed | tf_op | source)
XLA Modules:
  0.0 83.6 jit_solution(16329721097231656798)
XLA Ops:
  0.6 79.3 %shard_map.50 = (f32[96,128]{1,0:T(8,128)}, f32[1024,256]{1,0:T(8,128)}) custom-call(f32[96,128]{1,0:T(8,128)} %bitcast.17, f32[1024,256]{1,0:T(8,128)} %proto.1, s32[24576,128]{1,0:T(8,128)} %bitcast.16), custom_call_target="tpu_custom_call" | custom-call | flops 14495514624 | bytes 16777216 | tf_op jit(solution)/shard_map/pallas_call | solution.py:543
  79.9 1.4 %copy.10 = f32[24,2,256]{2,1,0:T(2,128)} copy(f32[24,2,256]{2,1,0:T(2,128)} %bitcast.15) | data formatting | bytes 98304
  81.3 2.3 %copy.11 = f32[1024,256]{1,0:T(8,128)} copy(f32[1024,256]{1,0:T(8,128)} %get-tuple-element.9) | data formatting | bytes 2097152

commit v3 on v2

--- a/solution.py
+++ b/solution.py
@@ -20,9 +20,9 @@
 ROWS = 8 * GRP
 ZN, XN = 8, 4
 
-ORDER = [0, 1, 7, 2, 6, 3, 5, 4]
+ORDER = [0, 2, 6, 3, 5, 1, 7, 4]
 POS = {dz: at for at, dz in enumerate(ORDER)}
-BACK = [4, 3, 5, 2, 6, 1, 7, 0]
+BACK = [4, 1, 7, 3, 5, 2, 6, 0]
 FAR = [4, 3, 5, 2, 6]
 
 _NAMES = (
@@ -171,7 +171,7 @@
     own_blk = blk[0, 0]
     for d in (1, 3, 2):
         send(own_blk, own_blk, "px%d" % d, xpeers[d - 1])
-    for d in (4, 3, 5, 2, 6, 1, 7):
+    for d in (2, 6, 3, 5, 4, 1, 7):
         send(own_blk, own_blk, "pz%d" % d, zpeers[d - 1])
 
     pro_copy.wait()
@@ -225,20 +225,18 @@
         arrive(theirs_of[dz], "s%d" % dz)
 
     def early_comm(i):
-        if i == 3:
+        if i == 2:
             relay_z()
-        elif i == 5:
-            relay_x(2), relay_x(6)
+        elif i == 4:
+            relay_x(6), relay_x(2)
         elif i == 6:
-            relay_x(3), relay_x(5)
+            relay_x(5), relay_x(3)
         elif i == 7:
             relay_x(4)
 
     def gather_comm(i):
-        if i == 0:
-            collect(1), collect(7)
-        elif i < 6:
-            collect(ORDER[i + 2])
+        if i < 7:
+            collect(ORDER[i + 1])
         use(ORDER[i])
 
     def codes(i, carry):
@@ -460,12 +458,8 @@
 
     def slab_comm(k):
         ystep(1, k)
-        if k == 0:
-            for dz in BACK[:7]:
-                sums_out(dz)
-        else:
-            if k >= 2:
-                ystep(2, k - 2)
+        if k >= 2:
+            ystep(2, k - 2)
 
     def column(group):
         cols = []
@@ -498,14 +492,18 @@
     backq = [zs[dz] for dz in BACK]
     lax.fori_loop(0, 8, backward, 0)
     lax.fori_loop(0, 8, weighted, 0)
+    for dz in BACK[:7]:
+        sums_out(dz)
     lax.fori_loop(0, 4, slab, 0)
 
     ystep(2, 2)
     ystep(3, 0)
     sums_here()
+    for dz in FAR[:3]:
+        sums_onward(dz)
     ystep(2, 3)
     ystep(3, 1)
-    for dz in FAR:
+    for dz in FAR[3:]:
         sums_onward(dz)
     ystep(3, 2)
     ystep(4, 0)
@@ -533,6 +531,11 @@
         make().wait_send()
     for s in range(4):
         out_copy(s).wait()
+
+
+def hand_over(fg, pg, fg_out, pg_out):
+    fg_out[...] = fg[...]
+    pg_out[...] = pg[...]
 
 
 def per_device(features, prototypes, code_counts):
@@ -584,6 +587,12 @@
         ),
         cost_estimate=pl.CostEstimate(flops=18 * ROWS * KL * D, bytes_accessed=16 << 20, transcendentals=ROWS * KL),
     )(feat, prototypes, counts)
+    fg, pg = pl.pallas_call(
+        hand_over,
+        out_shape=(jax.ShapeDtypeStruct((96, 128), F32), jax.ShapeDtypeStruct((KL, D), F32)),
+        in_specs=[vmem, vmem],
+        out_specs=(vmem, vmem),
+    )(fg, pg)
     features_grad = fg.reshape(24, 2, 2, 128).transpose(0, 2, 1, 3).reshape(24, 2, 256)
     return features_grad, pg
 

time: 84 us -> 81.5 us (0.970)
  local copies, waits for them, and re-layouts: 3.68 us -> 0 us
  Pallas kernels: 79.3 us -> 80.7 us
    unnamed x2 -> x0, local copies, waits for them, and re-layouts: 3.68 us -> none
    pallas_call x0 -> x1, Pallas kernels: none -> 2.3 us  [per_device(): pl.pallas_call(hand_over, out_shape=(jax.ShapeDtypeStruct((96, 128), F32)...]
where the time goes in v3:
time: 81.5 us; the launch traced here: 81.4 us
  Pallas kernels  80.7 us (99%)
    pallas_call x1, Pallas kernels, per_device(): pl.pallas_call(kernel, out_shape=(jax.ShapeDtypeStruct((96, 128), F32), j...  78.4 us
    pallas_call x1, Pallas kernels, per_device(): pl.pallas_call(hand_over, out_shape=(jax.ShapeDtypeStruct((96, 128), F32)...  2.3 us

profile of v3, /device:TPU:8, one launch (start us, length us, event | category | flops | bytes accessed | tf_op | source)
XLA Modules:
  0.0 81.4 jit_solution(2687608803294255468)
XLA Ops:
  0.6 78.4 %shard_map.50 = (f32[96,128]{1,0:T(8,128)}, f32[1024,256]{1,0:T(8,128)}) custom-call(f32[96,128]{1,0:T(8,128)} %bitcast.16, f32[1024,256]{1,0:T(8,128)} %proto.1, s32[24576,128]{1,0:T(8,128)} %bitcast.15), custom_call_target="tpu_custom_call" | custom-call | flops 14495514624 | bytes 16777216 | tf_op jit(solution)/shard_map/pallas_call | solution.py:546
  79.1 2.3 %shard_map.51 = (f32[96,128]{1,0:T(8,128)}, f32[1024,256]{1,0:T(8,128)}) custom-call(f32[96,128]{1,0:T(8,128)} %get-tuple-element.6.fg, f32[1024,256]{1,0:T(8,128)} %get-tuple-element.7.pg), custom_call_target="tpu_custom_call" | custom-call | tf_op jit(solution)/shard_map/pallas_call | solution.py:590

commit v4 on v3

--- a/solution.py
+++ b/solution.py
@@ -325,6 +325,7 @@
         copy.start()
     codes_slab(0)
     codes_slab(1)
+    lax.fori_loop(0, 1, forward_grad, 0)
     for copy in first:
         copy.wait()
     mine = tbuf[g8]
@@ -336,7 +337,7 @@
         copy.start()
     codes_slab(2)
     codes_slab(3)
-    lax.fori_loop(0, 2, forward_grad, 0)
+    lax.fori_loop(1, 4, forward_grad, 0)
     for copy in second:
         copy.wait()
     mine = t2[7]
@@ -346,7 +347,7 @@
     third = [small(t3.at[g8], t3.at[g8], t3s.at[k], t3r.at[k], peers[k]) for k in range(7)]
     for copy in third:
         copy.start()
-    lax.fori_loop(2, 8, forward_grad, 0)
+    lax.fori_loop(4, 8, forward_grad, 0)
     for k in range(7):
         small(t3.at[ranks[6 - k]], t3.at[ranks[6 - k]], t3s.at[k], t3r.at[k], peers[k]).wait_recv()
     for copy in third:

time: 81.5 us -> 81.2 us (level)
  no operation moved by 1% of the time
where the time goes in v4:
time: 81.2 us; the launch traced here: 81 us
  Pallas kernels  80.4 us (99%)
    pallas_call x1, Pallas kernels, per_device(): pl.pallas_call(kernel, out_shape=(jax.ShapeDtypeStruct((96, 128), F32), j...  78.1 us
    pallas_call x1, Pallas kernels, per_device(): pl.pallas_call(hand_over, out_shape=(jax.ShapeDtypeStruct((96, 128), F32)...  2.3 us

profile of v4, /device:TPU:8, one launch (start us, length us, event | category | flops | bytes accessed | tf_op | source)
XLA Modules:
  0.0 81.0 jit_solution(12834472492875478433)
XLA Ops:
  0.6 78.1 %shard_map.50 = (f32[96,128]{1,0:T(8,128)}, f32[1024,256]{1,0:T(8,128)}) custom-call(f32[96,128]{1,0:T(8,128)} %bitcast.16, f32[1024,256]{1,0:T(8,128)} %proto.1, s32[24576,128]{1,0:T(8,128)} %bitcast.15), custom_call_target="tpu_custom_call" | custom-call | flops 14495514624 | bytes 16777216 | tf_op jit(solution)/shard_map/pallas_call | solution.py:547
  78.8 2.3 %shard_map.51 = (f32[96,128]{1,0:T(8,128)}, f32[1024,256]{1,0:T(8,128)}) custom-call(f32[96,128]{1,0:T(8,128)} %get-tuple-element.6.fg, f32[1024,256]{1,0:T(8,128)} %get-tuple-element.7.pg), custom_call_target="tpu_custom_call" | custom-call | tf_op jit(solution)/shard_map/pallas_call | solution.py:591

commit v5 on v4

--- a/solution.py
+++ b/solution.py
@@ -512,6 +512,7 @@
     ystep(4, 1)
     ystep(4, 2)
     ystep(5, 0)
+    ystep(4, 3)
     sums_end()
 
     f, norm = load_features()
@@ -524,7 +525,6 @@
             piece = out[j * (BLK // 2) : (j + 1) * (BLK // 2), kt * 128 : (kt + 1) * 128]
             fg[pl.ds(kt * 2 + j, BLK // 2, stride=4), :] = piece
 
-    ystep(4, 3)
     ystep(5, 1)
     ystep(5, 2)
     ystep(5, 3)

time: 81.2 us -> 81.3 us (level)
  no operation moved by 1% of the time
where the time goes in v5:
time: 81.3 us; the launch traced here: 81.1 us
  Pallas kernels  80.5 us (99%)
    pallas_call x1, Pallas kernels, per_device(): pl.pallas_call(kernel, out_shape=(jax.ShapeDtypeStruct((96, 128), F32), j...  78.2 us
    pallas_call x1, Pallas kernels, per_device(): pl.pallas_call(hand_over, out_shape=(jax.ShapeDtypeStruct((96, 128), F32)...  2.3 us

profile of v5, /device:TPU:8, one launch (start us, length us, event | category | flops | bytes accessed | tf_op | source)
XLA Modules:
  0.0 81.1 jit_solution(8860621171240196566)
XLA Ops:
  0.6 78.2 %shard_map.50 = (f32[96,128]{1,0:T(8,128)}, f32[1024,256]{1,0:T(8,128)}) custom-call(f32[96,128]{1,0:T(8,128)} %bitcast.16, f32[1024,256]{1,0:T(8,128)} %proto.1, s32[24576,128]{1,0:T(8,128)} %bitcast.15), custom_call_target="tpu_custom_call" | custom-call | flops 14495514624 | bytes 16777216 | tf_op jit(solution)/shard_map/pallas_call | solution.py:547
  78.8 2.3 %shard_map.51 = (f32[96,128]{1,0:T(8,128)}, f32[1024,256]{1,0:T(8,128)}) custom-call(f32[96,128]{1,0:T(8,128)} %get-tuple-element.6.fg, f32[1024,256]{1,0:T(8,128)} %get-tuple-element.7.pg), custom_call_target="tpu_custom_call" | custom-call | tf_op jit(solution)/shard_map/pallas_call | solution.py:591
